TPU v7x, 32 devices: a whole 2x2x4 slice. The times are simulated.
32 devices in a mesh: dp: 16 (over z, y, x), context: 2 (over core).
Axes of the slice: x: 2, y: 2, z: 4, core: 2. Of those that a mesh axis runs over, the one named last changes fastest.
Arguments:
- hidden_in: bfloat16 [16, 256, 2048], P('dp', 'context'), may hold values from -6 to 6
- cotangent: bfloat16 [16, 256, 2048], P('dp', 'context'), may hold values from -6 to 6
- tile_depth: int32 [16, 2], P('dp'), may hold values from 1 to 4, as said below
- w_qkv: bfloat16 [3, 2048, 256], P(None, 'dp', 'context'), may hold values from -0.125 to 0.125
- w_out: bfloat16 [256, 2048], P('context', 'dp'), may hold values from -0.375 to 0.375
- gain: float32 [2048], replicated, may hold values from 0.1 to 1.9
Outputs:
- hidden_out: bfloat16 [16, 256, 2048], P('dp', 'context')
- grad_in: bfloat16 [16, 256, 2048], P('dp', 'context')
- grad_qkv: float32 [3, 2048, 256], P(None, 'dp', 'context')
- grad_out: float32 [256, 2048], P('context', 'dp')
Inputs may be any that keep to these rules, and one draw needn't show every extreme that they name: `tile_depth`: in every document at most 1 tiles have depth 2 or more and at most 1 have depth 3 or more; some document has exactly 1 and 1 such tiles.
All inputs are finite; a program needn't handle non-finite values.
Results may differ from a plain program's by a relative error of at most 0.028.
Values may be sent and summed in bfloat16 or wider, within the bound.
A program may use at most 64 MiB of HBM per device.

v0:
```python
import jax
import jax.numpy as jnp
from jax import lax
from jax.sharding import PartitionSpec as P

HD = 128


def from_root(value, axis, source):
    kept = jnp.where(lax.axis_index(axis) == source, value, 0).astype(value.dtype)
    return lax.psum(kept, axis)


def slot_plan(depth, level, cap, me):
    alive = depth >= level
    alive_int = alive.astype(jnp.int32)
    rank = jnp.cumsum(alive_int) - alive_int
    places = jnp.arange(depth.shape[0], dtype=jnp.int32)
    owners = [jnp.sum(jnp.where(alive & (rank == 0), places, 0))]
    valid = [jnp.any(alive & (rank == 0))]
    own_alive = jnp.any(alive & (places == me))
    own_slot = jnp.sum(jnp.where(places == me, jnp.minimum(rank, cap - 1), 0))
    return (owners, valid, own_alive, own_slot)


def gather_slots(tile_rows, owners, valid):
    pieces = []
    for owner, usable in zip(owners, valid):
        got = from_root(tile_rows, "context", owner)
        pieces.append(jnp.where(usable, got, jnp.zeros_like(got)))
    return pieces[0]


def head_sum(terms):
    return lax.psum(terms.astype(jnp.bfloat16), "context").astype(jnp.float32)


def forward_level(state, plan, full_qkv, full_out, gain):
    owners, valid, own_alive, own_slot = plan
    tile = state.shape[0]
    x32 = state.astype(jnp.float32)
    inv = lax.rsqrt(jnp.mean(x32 * x32, -1, keepdims=True) + 1e-06)
    normed = (x32 * inv * gain).astype(jnp.bfloat16)
    rows = gather_slots(normed, owners, valid)
    count = rows.shape[0]
    local_heads = full_qkv.shape[2] // HD
    qkv = jnp.einsum("rd,tdc->trc", rows, full_qkv, preferred_element_type=jnp.float32).astype(
        jnp.bfloat16
    )
    heads = qkv.reshape(3, count, local_heads, HD)
    query, key, value = (heads[0], heads[1], heads[2])
    valid_rows = jnp.repeat(jnp.stack(valid), tile)
    pos = jnp.arange(count)
    allowed = valid_rows[None, :] & (pos[None, :] <= pos[:, None])
    scores = jnp.einsum("qhd,khd->hqk", query, key, preferred_element_type=jnp.float32) * HD ** (
        -0.5
    )
    scores = jnp.where(allowed[None], scores, -1e30)
    top = jnp.max(scores, -1, keepdims=True)
    expo = jnp.exp(scores - top)
    prob = expo / jnp.sum(expo, -1, keepdims=True)
    probb = prob.astype(jnp.bfloat16)
    attn = jnp.einsum("hqk,khd->qhd", probb, value, preferred_element_type=jnp.float32).astype(
        jnp.bfloat16
    )
    attn_flat = attn.reshape(count, local_heads * HD)
    mixed = head_sum(jnp.dot(attn_flat, full_out, preferred_element_type=jnp.float32))
    new_state = (x32 + jnp.where(own_alive, mixed, jnp.zeros_like(mixed))).astype(jnp.bfloat16)
    return (new_state, (x32, inv, rows, query, key, value, prob, probb, attn, attn_flat))


def backward_level(grad_tile, keep, plan, full_qkv, full_out, gain):
    owners, valid, own_alive, own_slot = plan
    x32, inv, rows, query, key, value, prob, probb, attn, attn_flat = keep
    count = rows.shape[0]
    local_heads = query.shape[1]
    masked = jnp.where(own_alive, grad_tile, jnp.zeros_like(grad_tile))
    grad_rows = gather_slots(masked, owners, valid)
    dattn = jnp.einsum("rd,cd->rc", grad_rows, full_out, preferred_element_type=jnp.float32).astype(
        jnp.bfloat16
    )
    grad_wo = jnp.einsum("rc,rd->cd", attn_flat, grad_rows, preferred_element_type=jnp.float32)
    dheads = dattn.reshape(count, local_heads, HD)
    delta = jnp.sum(dheads.astype(jnp.float32) * attn.astype(jnp.float32), -1)
    dprob = jnp.einsum("qhd,khd->hqk", dheads, value, preferred_element_type=jnp.float32)
    dscore = (prob * (dprob - delta.T[:, :, None]) * HD ** (-0.5)).astype(jnp.bfloat16)
    d_query = jnp.einsum("hqk,khd->qhd", dscore, key, preferred_element_type=jnp.float32).astype(
        jnp.bfloat16
    )
    d_key = jnp.einsum("hqk,qhd->khd", dscore, query, preferred_element_type=jnp.float32).astype(
        jnp.bfloat16
    )
    d_value = jnp.einsum("hqk,qhd->khd", probb, dheads, preferred_element_type=jnp.float32).astype(
        jnp.bfloat16
    )
    dqkv = jnp.stack([d_query, d_key, d_value]).reshape(3, count, local_heads * HD)
    grad_wqkv = jnp.einsum("rd,trc->tdc", rows, dqkv, preferred_element_type=jnp.float32)
    dnorm = head_sum(jnp.einsum("trc,tdc->rd", dqkv, full_qkv, preferred_element_type=jnp.float32))
    scaled = dnorm * gain
    dx = inv * scaled - x32 * inv**3 * jnp.mean(x32 * scaled, -1, keepdims=True)
    dx = jnp.where(own_alive, dx, jnp.zeros_like(dx))
    new_grad = (grad_tile.astype(jnp.float32) + dx).astype(jnp.bfloat16)
    return (new_grad, grad_wqkv, grad_wo)


def on_device(hidden_in, cotangent, tile_depth, w_qkv, w_out, gain):
    count = lax.axis_size("context")
    me = lax.axis_index("context")
    depth = tile_depth[0]
    plans = [
        slot_plan(depth, 2, max(1, count // 8), me),
        slot_plan(depth, 3, max(1, count // 16), me),
    ]
    full_qkv, full_out = (
        lax.all_gather(w_qkv, "dp", axis=1, tiled=True),
        lax.all_gather(w_out, "dp", axis=1, tiled=True),
    )
    state = hidden_in[0]
    saved = []
    for plan in plans:
        state, keep = forward_level(state, plan, full_qkv, full_out, gain)
        saved.append(keep)
    back_qkv, back_out = (
        lax.all_gather(w_qkv, "dp", axis=1, tiled=True),
        lax.all_gather(w_out, "dp", axis=1, tiled=True),
    )
    grad_state = cotangent[0]
    total_qkv = jnp.zeros(full_qkv.shape, jnp.float32)
    total_out = jnp.zeros(full_out.shape, jnp.float32)
    for index in (1, 0):
        grad_state, part_qkv, part_out = backward_level(
            grad_state, saved[index], plans[index], back_qkv, back_out, gain
        )
        total_qkv = total_qkv + part_qkv
        total_out = total_out + part_out
    shard_qkv, shard_out = (
        lax.psum_scatter(total_qkv, "dp", scatter_dimension=1, tiled=True),
        lax.psum_scatter(total_out, "dp", scatter_dimension=1, tiled=True),
    )
    return (state[None], grad_state[None], shard_qkv, shard_out)


def solution(mesh):
    in_specs = (
        P("dp", "context", None),
        P("dp", "context", None),
        P("dp", None),
        P(None, "dp", "context"),
        P("context", "dp"),
        P(),
    )
    out_specs = (
        P("dp", "context", None),
        P("dp", "context", None),
        P(None, "dp", "context"),
        P("context", "dp"),
    )
    return jax.shard_map(
        on_device, mesh=mesh, in_specs=in_specs, out_specs=out_specs, check_vma=False
    )
```

profile of v0, /device:TPU:0, one launch (start us, length us, event | category | flops | bytes accessed | tf_op | source)
XLA Modules:
  0.0 405.6 jit_solution(16461162913929824545)
XLA Ops:
  8.1 1.2 fusion.28
  10.3 1.4 fusion.91
  13.0 2.1 fusion.39
  15.7 46.0 %all_gather.9 = bf16[128,2048]{1,0:T(8,128)(2,1)S(1)} all-gather(bf16[128,128]{1,0:T(8,128)(2,1)S(1)} %copy-done.10), channel_id=1, replica_groups=mesh['dp'=16,'context'=2] {'dp'}, dimensions={1}, use_global_device_ids=true | all-gather | bytes 557056 | tf_op jit(solution)/shard_map/all_gather | solution.py:116
  61.7 18.6 %all-gather.2.cloned.1.call-done = bf16[3,2048,128]{2,1,0:T(8,128)(2,1)} async-done(((bf16[3,128,128]{2,1,0:T(8,128)(2,1)}), bf16[3,2048,128]{2,1,0:T(8,128)(2,1)}) %all-gather.2.cloned.1.call-update) | async-done | bytes 1572880 | tf_op jit(solution)/shard_map/all_gather | solution.py:115
  80.3 2.7 fusion.2
  84.2 1.1 convolution_convert_fusion.1
  86.7 1.5 select_bitcast_fusion
  88.1 14.7 %all-reduce.11.cloned.1.call-done = bf16[128,2048]{1,0:T(8,128)(2,1)} async-done(((bf16[128,2048]{1,0:T(8,128)(2,1)}), bf16[128,2048]{1,0:T(8,128)(2,1)}) %all-reduce.11.cloned.1.call-update) | async-done | bytes 524304 | tf_op jit(solution)/shard_map/psum | solution.py:35
  102.9 2.1 fusion.18
  105.0 1.0 fusion.41
  106.1 21.0 %all-reduce.19.cloned.1.call-done = (bf16[128,2048]{1,0:T(8,128)(2,1)}, bf16[128,2048]{1,0:T(8,128)(2,1)}) async-done(((bf16[128,2048]{1,0:T(8,128)(2,1)}, bf16[128,2048]{1,0:T(8,128)(2,1)}), (bf16[128,2048]{1,0:T(8,128)(2,1)}, bf16[128,2048]{1,0:T(8,128)(2,1)})) %all-reduce.19.cloned.1.call-update) | async-done | bytes 1048592 | tf_op jit(solution)/shard_map/psum | solution.py:11
  127.1 1.1 fusion.3
  129.3 1.0 fusion.57
  131.0 1.5 fusion
  132.5 20.0 %all-reduce.13.cloned.1.call-done = bf16[128,2048]{1,0:T(8,128)(2,1)} async-done(((bf16[128,2048]{1,0:T(8,128)(2,1)}), bf16[128,2048]{1,0:T(8,128)(2,1)}) %all-reduce.13.cloned.1.call-update) | async-done | bytes 524304 | tf_op jit(solution)/shard_map/psum | solution.py:35
  152.5 1.3 fusion.27
  153.8 4.1 select_select_fusion
  158.0 1.1 convolution_convert_fusion
  159.1 18.9 %all-reduce.15.cloned.1.call-done = bf16[128,2048]{1,0:T(8,128)(2,1)} async-done(((bf16[128,2048]{1,0:T(8,128)(2,1)}), bf16[128,2048]{1,0:T(8,128)(2,1)}) %all-reduce.15.cloned.1.call-update) | async-done | bytes 524304 | tf_op jit(solution)/shard_map/psum | solution.py:11
  178.0 2.0 fusion.56
  180.7 1.5 fusion.1
  182.2 1.3 fusion.42
  183.5 2.9 add_bitcast_fusion
  186.5 1.0 copy-done.5
  188.4 1.9 convolution_add_fusion
  190.3 11.8 %all-reduce.17.cloned.1.call-done = (bf16[128,2048]{1,0:T(8,128)(2,1)}, bf16[128,2048]{1,0:T(8,128)(2,1)}) async-done(((bf16[128,2048]{1,0:T(8,128)(2,1)}, bf16[128,2048]{1,0:T(8,128)(2,1)}), (bf16[128,2048]{1,0:T(8,128)(2,1)}, bf16[128,2048]{1,0:T(8,128)(2,1)})) %all-reduce.17.cloned.1.call-update) | async-done | bytes 1048592 | tf_op jit(solution)/shard_map/psum | solution.py:35
  202.1 1.3 fusion.37
  203.4 4.2 %fusion.38 = (bf16[1,128,2048]{2,1,0:T(8,128)(2,1)}, bf16[1,128,2048]{2,1,0:T(8,128)(2,1)}) fusion(bf16[128,2048]{1,0:T(8,128)(2,1)} %get-tuple-element.11, bf16[128,2048]{1,0:T(8,128)(2,1)S(1)} %copy-done.3, bf16[1,128,2048]{2,1,0:T(8,128)(2,1)S(1)} %copy-done, f32[128]{0:T(128)S(1)} %broadcast_multiply_fusion, f32[128]{0:T(128)S(1)} %get-tuple-element.22, ...), kind=kLoop, calls=%fused_computation.72 | loop fusion | flops 4194304 | bytes 3679746 | tf_op jit(solution)/shard_map/broadcast_in_dim | solution.py:140
  207.6 110.7 %reduce-scatter.3.cloned.1.call-done = f32[3,128,128]{1,2,0:T(8,128)} async-done(((f32[3,2048,128]{1,2,0:T(8,128)}), f32[3,128,128]{1,2,0:T(8,128)}) %reduce-scatter.3.cloned.1.call-update) | async-done | bytes 196624 | tf_op jit(solution)/shard_map/reduce_scatter | solution.py:137
  318.3 1.7 copy.14
  320.0 78.0 %reduce-scatter.5.cloned.1.call-done = f32[128,128]{1,0:T(8,128)} async-done(((f32[128,2048]{1,0:T(8,128)}), f32[128,128]{1,0:T(8,128)}) %reduce-scatter.5.cloned.1.call-update) | async-done | bytes 65552 | tf_op jit(solution)/shard_map/reduce_scatter | solution.py:138
  (64 shorter events, 7.9 us)
Async XLA Ops:
  8.0 7.7 %copy-start.10 = (bf16[128,128]{1,0:T(8,128)(2,1)S(1)}, bf16[128,128]{1,0:T(8,128)(2,1)}, u32[]{:S(2)}) copy-start(bf16[128,128]{1,0:T(8,128)(2,1)} %param.10) | copy-start | bytes 98308
  8.0 53.7 %all-reduce.9.cloned.1.call-start = ((), (), s32[]{:S(2)}) async-start(), calls=%async_computation.2 | async-start | bytes 1048576 | tf_op jit(solution)/shard_map/psum | solution.py:11
  15.1 65.3 %all-gather.2.cloned.1.call-start = ((), (), s32[]{:S(2)}) async-start(), calls=%async_computation.3 | async-start | bytes 1671168 | tf_op jit(solution)/shard_map/all_gather | solution.py:115
  15.7 87.2 %all-reduce.11.cloned.1.call-start = ((), (), s32[]{:S(2)}) async-start(), calls=%async_computation.4 | async-start | bytes 1048576 | tf_op jit(solution)/shard_map/psum | solution.py:35
  83.0 3.7 copy-start.2
  83.0 19.9 %copy-start = (bf16[1,128,2048]{2,1,0:T(8,128)(2,1)S(1)}, bf16[1,128,2048]{2,1,0:T(8,128)(2,1)}, u32[]{:S(2)}) copy-start(bf16[1,128,2048]{2,1,0:T(8,128)(2,1)} %param.6) | copy-start | bytes 1572868
  85.3 19.7 %copy-start.9 = (f32[2048]{0:T(1024)S(1)}, f32[2048]{0:T(1024)}, u32[]{:S(2)}) copy-start(f32[2048]{0:T(1024)} %param.11) | copy-start | bytes 24580
  85.3 41.7 %all-reduce.19.cloned.1.call-start = ((), (), s32[]{:S(2)}) async-start(), calls=%async_computation.10 | async-start | bytes 2097152 | tf_op jit(solution)/shard_map/psum | solution.py:11
  102.9 24.2 %copy-start.1 = (bf16[3,2048,128]{2,1,0:T(8,128)(2,1)S(1)}, bf16[3,2048,128]{2,1,0:T(8,128)(2,1)}, u32[]{:S(2)}) copy-start(bf16[3,2048,128]{2,1,0:T(8,128)(2,1)} %all-gather.2.cloned.1.call-done) | copy-start | bytes 4718596
  106.1 46.5 %all-reduce.13.cloned.1.call-start = ((), (), s32[]{:S(2)}) async-start(), calls=%async_computation.5 | async-start | bytes 1048576 | tf_op jit(solution)/shard_map/psum | solution.py:35
  127.1 2.2 copy-start.4
  132.5 45.5 %all-reduce.15.cloned.1.call-start = ((), (), s32[]{:S(2)}) async-start(), calls=%async_computation.6 | async-start | bytes 1048576 | tf_op jit(solution)/shard_map/psum | solution.py:11
  157.9 44.2 %all-reduce.17.cloned.1.call-start = ((), (), s32[]{:S(2)}) async-start(), calls=%async_computation.9 | async-start | bytes 2097152 | tf_op jit(solution)/shard_map/psum | solution.py:35
  180.7 1.6 copy-start.6
  182.2 1.3 copy-start.8
  182.2 136.1 %reduce-scatter.3.cloned.1.call-start = ((), (), s32[]{:S(2)}) async-start(), calls=%async_computation.7 | async-start | bytes 3342336 | tf_op jit(solution)/shard_map/reduce_scatter | solution.py:137
  186.4 1.0 copy-start.5
  186.4 2.0 copy-start.7
  186.4 211.6 %reduce-scatter.5.cloned.1.call-start = ((), (), s32[]{:S(2)}) async-start(), calls=%async_computation.8 | async-start | bytes 1114112 | tf_op jit(solution)/shard_map/reduce_scatter | solution.py:138
  190.3 13.1 %copy-start.3 = (bf16[128,2048]{1,0:T(8,128)(2,1)S(1)}, bf16[128,2048]{1,0:T(8,128)(2,1)}, u32[]{:S(2)}) copy-start(bf16[128,2048]{1,0:T(8,128)(2,1)} %get-tuple-element.15) | copy-start | bytes 1572868
Sparse Core Ops, SparseCore 0:
  15.2 21.4 all-reduce.8
  85.4 17.4 all-reduce.10
  106.2 20.8 all-reduce.18
  132.6 19.9 all-reduce.12
  158.0 19.8 all-reduce.14
  182.3 19.7 all-reduce.16
Sparse Core Ops, SparseCore 1:
  18.7 61.6 all-gather.1
  187.6 130.6 reduce-scatter.2
  321.0 76.9 reduce-scatter.4
where the time goes:
time: 408 us; the launch traced here: 406 us
  waiting for transfers between devices  294 us (72%)
  blocking collectives  46 us (11%)
  other arithmetic  22.5 us (6%)
  matrix products  22.4 us (5%)
  between operations  17.3 us (4%)
    reduce_scatter x1, waiting for transfers between devices, on_device(): lax.psum_scatter(total_qkv, 'dp', scatter_dimension=1, tiled=True)  111 us
    reduce_scatter x1, waiting for transfers between devices, on_device(): lax.psum_scatter(total_out, 'dp', scatter_dimension=1, tiled=True)  78 us
    psum x3, waiting for transfers between devices, head_sum(): return lax.psum(terms.astype(jnp.bfloat16), 'context').astype(jnp.float32)  46.6 us
    all_gather x1, blocking collectives, on_device(): lax.all_gather(w_out, 'dp', axis=1, tiled=True)  46 us
    psum x3, waiting for transfers between devices, from_root(): return lax.psum(kept, axis)  39.8 us
    all_gather x1, waiting for transfers between devices, on_device(): lax.all_gather(w_qkv, 'dp', axis=1, tiled=True)  18.6 us
    select_n x4, other arithmetic, from_root(): jnp.where(lax.axis_index(axis) == source, value, 0).astype(value.dtype)  8.61 us
  transfers between devices with their start and end apart: 9, of which 8 were waited for; matrix products, arithmetic and copies ran while one was open for 4% of the time, Pallas kernels for 0%

commit v1 on v0

v1 whole, which is shorter than its diff:
```python
import functools

import jax
import jax.numpy as jnp
from jax import lax
from jax.experimental import pallas as pl
from jax.experimental.pallas import tpu as pltpu
from jax.sharding import PartitionSpec as P

HD = 128
MESH = pl.DeviceIdType.MESH
BF = jnp.bfloat16
F32 = jnp.float32
EXCHANGES = ("mix2", "mix3", "dn3", "dn2")


def grid_of(n):
    if n == 64:
        return (16, 4, 1)
    if n % 4 == 0:
        return (n // 4, 2, 2)
    return (n, 1, 1)


def copy_keys(dims, contexts, chunks):
    Z, Y, X = dims
    first = (X, Y)
    second = (Y, X)
    keys = []
    for o in range(1, contexts):
        keys += [("hid", o), ("cot", o)]
        keys += [(name, o, j) for name in EXCHANGES for j in range(chunks)]
    for h in range(2):
        keys += [("gz", h, oz) for oz in range(1, Z)]
        keys += [("g1", h, o1, oz) for o1 in range(1, first[h]) for oz in range(Z)]
        keys += [
            ("g2", h, o2, o1, oz)
            for o2 in range(1, second[h])
            for o1 in range(first[h])
            for oz in range(Z)
        ]
        keys += [
            ("s1", h, o1, o2, oz)
            for o1 in range(1, second[h])
            for o2 in range(first[h])
            for oz in range(Z)
        ]
        keys += [("s2", h, o2, oz) for o2 in range(1, first[h]) for oz in range(Z)]
        keys += [("s3", h, oz) for oz in range(1, Z)]
    return {key: number for number, key in enumerate(keys)}


def nn(a, b):
    return jnp.dot(a, b, preferred_element_type=F32)


def nt(a, b):
    return lax.dot_general(a, b, (((1,), (1,)), ((), ())), preferred_element_type=F32)


def kernel(
    dims, contexts, chunks, keys,
    depth, hid, cot, wq, wo, gain,
    hout, gout, gqkv, gwo,
    WA, WB, WAT, WBT, accA, accB, peer_h, peer_g, hL, h2, R, DY, scaled, own_x, got_x,
    G, R1a, R1b, R2a, R2b, R3, T1a, T1b, T2, send_sem, recv_sem,
):
    Z, Y, X = dims
    dp = lax.axis_index("dp")
    ctx = lax.axis_index("context")
    zz, yy, xx = dp // (Y * X), lax.rem(dp // X, Y), lax.rem(dp, X)
    tile, D = hid.shape[1], hid.shape[2]
    dloc = wq.shape[1]
    width = D // chunks
    me = (zz, yy, xx)
    order = ((2, 1), (1, 2))

    def spot(**moves):
        place = list(me)
        for name, off in moves.items():
            axis = int(name[1])
            place[axis] = lax.rem(me[axis] + off + dims[axis], dims[axis]) if off else me[axis]
        return (place[0] * Y + place[1]) * X + place[2]

    def at(axes):
        return spot(**{"a%d" % axis: off for axis, off in axes})

    started = []

    def copy(key, src, dst, peer):
        number = keys[key]
        return pltpu.make_async_remote_copy(
            src_ref=src, dst_ref=dst, send_sem=send_sem.at[number], recv_sem=recv_sem.at[number],
            device_id=peer, device_id_type=MESH,
        )

    def send(key, src, dst, peer):
        c = copy(key, src, dst, peer)
        c.start()
        started.append(c)

    def arrive(key, dst):
        copy(key, dst, dst, (dp, ctx)).wait_recv()

    def ctx_peer(o):
        return (dp, lax.rem(ctx + o, contexts))

    barrier = pltpu.get_barrier_semaphore()
    peers = [(at([(axis, o)]), ctx) for axis in range(3) for o in range(1, dims[axis])]
    peers += [ctx_peer(o) for o in range(1, contexts)]
    for peer in peers:
        pl.semaphore_signal(barrier, inc=1, device_id=peer, device_id_type=MESH)

    mine = pl.ds(pl.multiple_of(dp * dloc, dloc), dloc)
    WA[mine, 0:HD] = wq[0]
    WA[mine, HD : 2 * HD] = wq[1]
    WB[mine, 0:HD] = wq[2]
    WB[mine, HD : 2 * HD] = wo[...].T
    pl.semaphore_wait(barrier, len(peers))

    halves = (WA, WB)

    def piece(h, axes):
        p = at(axes)
        return halves[h].at[pl.ds(pl.multiple_of(p * dloc, dloc), dloc), :]

    for h in range(2):
        for oz in range(1, Z):
            block = piece(h, [])
            send(("gz", h, oz), block, block, (at([(0, oz)]), ctx))
    for o in range(1, contexts):
        slot = contexts - o - 1
        send(("hid", o), hid.at[0], peer_h.at[slot], ctx_peer(o))
        send(("cot", o), cot.at[0], peer_g.at[slot], ctx_peer(o))

    def spread_first(h, oz):
        d1 = order[h][0]
        block = piece(h, [(0, -oz)])
        for o1 in range(1, dims[d1]):
            send(("g1", h, o1, oz), block, block, (at([(d1, o1)]), ctx))

    def spread_second(h, oz, o1):
        d1, d2 = order[h]
        block = piece(h, [(0, -oz), (d1, -o1)])
        if o1:
            arrive(("g1", h, o1, oz), block)
        for o2 in range(1, dims[d2]):
            send(("g2", h, o2, o1, oz), block, block, (at([(d2, o2)]), ctx))

    def pass_on(oz):
        for h in range(2):
            for o1 in range(1, dims[order[h][0]]):
                spread_second(h, oz, o1)

    for h in range(2):
        spread_first(h, 0)
    for h in range(2):
        spread_second(h, 0, 0)

    tiles = depth.shape[1]

    def flag(level, place):
        return jnp.where(depth[0, place] >= level, 1.0, 0.0).astype(F32)

    def of(level, who):
        return sum(jnp.where(who == t, flag(level, t), 0.0) for t in range(tiles))

    own2 = of(2, ctx)
    valid2 = sum(flag(2, t) for t in range(tiles))
    valid3 = sum(flag(3, t) for t in range(tiles))
    for o in range(1, contexts):
        slot = contexts - o - 1
        arrive(("hid", o), peer_h.at[slot])
        arrive(("cot", o), peer_g.at[slot])
    cols = [pl.ds(j * width, width) for j in range(chunks)]
    square = jnp.zeros((tile, 1), F32)
    for c in cols:
        live_h = hid[0, :, c].astype(F32) * own2
        live_g = cot[0, :, c].astype(F32) * own2
        for s in range(contexts - 1):
            flag_s = of(2, lax.rem(ctx + s + 1, contexts))
            live_h = live_h + peer_h[s, :, c].astype(F32) * flag_s
            live_g = live_g + peer_g[s, :, c].astype(F32) * flag_s
        hL[:, c] = live_h.astype(BF)
        DY[0:tile, c] = live_g.astype(BF)
        DY[tile : 2 * tile, c] = (live_g * valid3).astype(BF)
        square = square + jnp.sum(live_h * live_h, -1, keepdims=True)
    inv2 = lax.rsqrt(square * (1.0 / D) + 1e-06)
    for c in cols:
        R[0:tile, c] = (hL[:, c].astype(F32) * inv2 * gain[:, c]).astype(BF)

    for oz in range(1, Z):
        for h in range(2):
            arrive(("gz", h, oz), piece(h, [(0, -oz)]))
            spread_first(h, oz)
        for h in range(2):
            spread_second(h, oz, 0)
        pass_on(oz - 1)
    pass_on(Z - 1)

    group = D // Z

    def group_of(oz):
        return pl.ds(pl.multiple_of(lax.rem(zz + oz + Z, Z) * group, group), group)

    for oz in range(Z):
        for h in range(2):
            d1, d2 = order[h]
            for o1 in range(dims[d1]):
                for o2 in range(1, dims[d2]):
                    arrive(("g2", h, o2, o1, oz), piece(h, [(0, -oz), (d1, -o1), (d2, -o2)]))
        g = group_of(-oz)
        rows, grads = R[0:tile, g], DY[0:tile, g]
        part_a = nn(rows, WA[g, :])
        part_b = nn(jnp.concatenate([rows, grads], axis=0), WB[g, :])
        accA[...] = part_a if oz == 0 else accA[...] + part_a
        accB[...] = part_b if oz == 0 else accB[...] + part_b
        WAT[:, g] = WA[g, :].T
        WBT[:, g] = WB[g, :].T

    causal = lax.broadcasted_iota(jnp.int32, (tile, tile), 1) <= lax.broadcasted_iota(
        jnp.int32, (tile, tile), 0
    )
    scale = HD ** (-0.5)

    def attend(qk, value, valid):
        allowed = causal & (jnp.broadcast_to(valid, causal.shape) > 0.5)
        qk, value = qk.astype(BF), value.astype(BF)
        query, key = qk[:, 0:HD], qk[:, HD : 2 * HD]
        scores = jnp.where(allowed, nt(query, key) * scale, -1e30)
        expo = jnp.exp(scores - jnp.max(scores, -1, keepdims=True))
        prob = expo / jnp.sum(expo, -1, keepdims=True)
        probb = prob.astype(BF)
        attn = nn(probb, value).astype(BF)
        return query, key, value, prob, probb, attn

    def swap_out(name, term):
        e = EXCHANGES.index(name)
        for j in range(chunks):
            own_x[e, j] = term(cols[j]).astype(BF)
            for o in range(1, contexts):
                send((name, o, j), own_x.at[e, j], got_x.at[e, contexts - o - 1, j], ctx_peer(o))

    def swap_in(name, j):
        e = EXCHANGES.index(name)
        total = own_x[e, j].astype(F32)
        for o in range(1, contexts):
            slot = contexts - o - 1
            arrive((name, o, j), got_x.at[e, slot, j])
            total = total + got_x[e, slot, j].astype(F32)
        return total

    def backward(keep, dattn):
        query, key, value, prob, probb, attn = keep
        delta = jnp.sum(dattn.astype(F32) * attn.astype(F32), -1, keepdims=True)
        dscore = (prob * (nt(dattn, value) - delta) * scale).astype(BF)
        dq = nn(dscore, key).astype(BF)
        dk = nn(dscore.T, query).astype(BF)
        dv = nn(probb.T, dattn).astype(BF)
        return jnp.concatenate([dq, dk], axis=1), dv

    keep2 = attend(accA[...], accB[0:tile, 0:HD], valid2)
    swap_out("mix2", lambda c: nn(keep2[5], WBT[HD : 2 * HD, c]))
    grad_out3 = accB[tile : 2 * tile, HD : 2 * HD]
    dattn3 = (grad_out3 * valid3).astype(BF)
    square = jnp.zeros((tile, 1), F32)
    qk3 = jnp.zeros((tile, 2 * HD), F32)
    vo3 = jnp.zeros((2 * tile, 2 * HD), F32)
    for j, c in enumerate(cols):
        state = (hL[:, c].astype(F32) + swap_in("mix2", j)).astype(BF)
        h2[:, c] = state
        wide = state.astype(F32)
        square = square + jnp.sum(wide * wide, -1, keepdims=True)
        gained = (wide * gain[:, c]).astype(BF)
        qk3 = qk3 + nn(gained, WA[c, :])
        vo3 = vo3 + nn(jnp.concatenate([gained, state], axis=0), WB[c, :])
    inv3 = lax.rsqrt(square * (1.0 / D) + 1e-06)
    state_out = vo3[tile : 2 * tile, HD : 2 * HD]

    factor3 = inv3 * valid3
    keep3 = attend(qk3 * factor3, vo3[0:tile, 0:HD] * factor3, valid3)
    dqk3, dv3 = backward(keep3, dattn3)
    swap_out("dn3", lambda c: nn(dqk3, WAT[:, c]) + nn(dv3, WBT[0:HD, c]))
    swap_out("mix3", lambda c: nn(keep3[5], WBT[HD : 2 * HD, c]))
    for c in cols:
        R[tile : 2 * tile, c] = (h2[:, c].astype(F32) * inv3 * gain[:, c] * valid3).astype(BF)

    def norm_grad(name, state, inv, on, term):
        dot = jnp.zeros((tile, 1), F32)
        for j, c in enumerate(cols):
            u = swap_in(name, j) * gain[:, c]
            scaled[:, c] = u
            dot = dot + jnp.sum(u * state[:, c].astype(F32), -1, keepdims=True)
            term(c, u)
        return inv * on, inv * inv * inv * (dot * (1.0 / D)) * on

    def norm_apply(state, c, first, second):
        return scaled[:, c] * first - state[:, c].astype(F32) * second

    back = [jnp.zeros((tile, HD), F32)]

    def back_term(c, u):
        back[0] = back[0] + nn(u.astype(BF), WB[c, HD : 2 * HD])

    first, second = norm_grad("dn3", h2, inv3, valid3, back_term)
    dattn2 = (grad_out3 + back[0] * first - state_out * second).astype(BF)
    dqk2, dv2 = backward(keep2, dattn2)
    for c in cols:
        DY[0:tile, c] = (DY[0:tile, c].astype(F32) + norm_apply(h2, c, first, second)).astype(BF)

    left_a = jnp.concatenate([dqk2, dqk3], axis=0).T
    left_v = jnp.concatenate([dv2, dv3], axis=0).T
    left_o = jnp.concatenate([keep2[5], keep3[5]], axis=0).T
    plane = Y * X

    def cut(rows, block, z):
        for i in range(plane):
            G[z * plane + i, rows, :] = block[:, i * dloc : (i + 1) * dloc].astype(BF)

    got1, got2, sum1 = (R1a, R1b), (R2a, R2b), (T1a, T1b)

    def half_rows(h):
        return pl.ds(h * 2 * HD, 2 * HD)

    for oz in (*range(1, Z), 0):
        g = group_of(oz)
        z = lax.rem(zz + oz, Z)
        cut(pl.ds(0, 2 * HD), nn(left_a, R[:, g]), z)
        cut(pl.ds(2 * HD, HD), nn(left_v, R[:, g]), z)
        cut(pl.ds(3 * HD, HD), nn(left_o, DY[:, g]), z)
        for o2 in reversed(range(max(X, Y))):
            for h in range(2):
                e2, e1 = order[h]
                for o1 in range(1, dims[e1] if o2 < dims[e2] else 1):
                    send(
                        ("s1", h, o1, o2, oz),
                        G.at[at([(0, oz), (e1, o1), (e2, o2)]), half_rows(h), :],
                        got1[h].at[o1 - 1, o2, oz],
                        (at([(e1, o1)]), ctx),
                    )
    swap_out("dn2", lambda c: nn(dqk2, WAT[:, c]) + nn(dv2, WBT[0:HD, c]))

    not2 = 1.0 - own2
    for j, c in enumerate(cols):
        state = (h2[:, c].astype(F32) + swap_in("mix3", j)).astype(BF).astype(F32)
        hout[0, :, c] = (hid[0, :, c].astype(F32) * not2 + state * own2).astype(BF)

    def first_total(h, o2, oz):
        e2, e1 = order[h]
        total = G[at([(0, oz), (e2, o2)]), half_rows(h), :].astype(F32)
        for o1 in range(1, dims[e1]):
            arrive(("s1", h, o1, o2, oz), got1[h].at[o1 - 1, o2, oz])
            total = total + got1[h][o1 - 1, o2, oz].astype(F32)
        return total

    for oz in (*range(1, Z), 0):
        for h in range(2):
            e2, e1 = order[h]
            for o2 in range(1, dims[e2]):
                sum1[h][o2 - 1, oz] = first_total(h, o2, oz).astype(BF)
                send(
                    ("s2", h, o2, oz), sum1[h].at[o2 - 1, oz], got2[h].at[o2 - 1, oz],
                    (at([(e2, o2)]), ctx),
                )

    first, second = norm_grad("dn2", hL, inv2, 1.0, lambda c, u: None)
    for c in cols:
        grad = DY[0:tile, c].astype(F32) + norm_apply(hL, c, first, second)
        grad = grad.astype(BF).astype(F32)
        gout[0, :, c] = (cot[0, :, c].astype(F32) * not2 + grad * own2).astype(BF)

    def second_total(h, oz):
        total = first_total(h, 0, oz)
        for o2 in range(1, dims[order[h][0]]):
            arrive(("s2", h, o2, oz), got2[h].at[o2 - 1, oz])
            total = total + got2[h][o2 - 1, oz].astype(F32)
        return total

    for oz in range(1, Z):
        for h in range(2):
            T2[h, oz - 1] = second_total(h, oz).astype(BF)
            send(("s3", h, oz), T2.at[h, oz - 1], R3.at[h, oz - 1], (at([(0, oz)]), ctx))
    final = [second_total(h, 0) for h in range(2)]
    for h in range(2):
        for oz in range(1, Z):
            arrive(("s3", h, oz), R3.at[h, oz - 1])
            final[h] = final[h] + R3[h, oz - 1].astype(F32)
    gqkv[0] = final[0][0:HD].T
    gqkv[1] = final[0][HD : 2 * HD].T
    gqkv[2] = final[1][0:HD].T
    gwo[...] = final[1][HD : 2 * HD]

    for c in started:
        c.wait_send()


def write_out(parts, *refs):
    sources, targets, sems = refs[:4], refs[4:8], refs[8]
    copies = []
    for number, (i, part) in enumerate(parts):
        index = (0, part) if i < 2 else part
        copies.append(
            pltpu.make_async_copy(sources[i].at[index], targets[i].at[index], sems.at[number])
        )
    for c in copies:
        c.start()
    for c in copies:
        c.wait()


def on_device(hidden_in, cotangent, tile_depth, w_qkv, w_out, gain):
    contexts = lax.axis_size("context")
    n = lax.axis_size("dp")
    dims = grid_of(n)
    Z, Y, X = dims
    _, tile, D = hidden_in.shape
    dloc = w_qkv.shape[1]
    chunks = 4
    width = D // chunks
    keys = copy_keys(dims, contexts, chunks)
    others = max(1, contexts - 1)
    vmem = pl.BlockSpec(memory_space=pltpu.VMEM)

    def block(*lead):
        return pltpu.VMEM((*[max(1, v) for v in lead], 2 * HD, dloc), BF)

    results = pl.pallas_call(
        functools.partial(kernel, dims, contexts, chunks, keys),
        out_shape=(
            jax.ShapeDtypeStruct(hidden_in.shape, BF),
            jax.ShapeDtypeStruct(cotangent.shape, BF),
            jax.ShapeDtypeStruct(w_qkv.shape, F32),
            jax.ShapeDtypeStruct(w_out.shape, F32),
        ),
        in_specs=[pl.BlockSpec(memory_space=pltpu.SMEM)] + [vmem] * 5,
        out_specs=(vmem,) * 4,
        scratch_shapes=[
            pltpu.VMEM((D, 2 * HD), BF),
            pltpu.VMEM((D, 2 * HD), BF),
            pltpu.VMEM((2 * HD, D), BF),
            pltpu.VMEM((2 * HD, D), BF),
            pltpu.VMEM((tile, 2 * HD), F32),
            pltpu.VMEM((2 * tile, 2 * HD), F32),
            pltpu.VMEM((others, tile, D), BF),
            pltpu.VMEM((others, tile, D), BF),
            pltpu.VMEM((tile, D), BF),
            pltpu.VMEM((tile, D), BF),
            pltpu.VMEM((2 * tile, D), BF),
            pltpu.VMEM((2 * tile, D), BF),
            pltpu.VMEM((tile, D), F32),
            pltpu.VMEM((len(EXCHANGES), chunks, tile, width), BF),
            pltpu.VMEM((len(EXCHANGES), others, chunks, tile, width), BF),
            pltpu.VMEM((n, 4 * HD, dloc), BF),
            block(Y - 1, X, Z),
            block(X - 1, Y, Z),
            block(X - 1, Z),
            block(Y - 1, Z),
            block(2, Z - 1),
            block(X - 1, Z),
            block(Y - 1, Z),
            block(2, Z - 1),
            pltpu.SemaphoreType.DMA((len(keys),)),
            pltpu.SemaphoreType.DMA((len(keys),)),
        ],
        compiler_params=pltpu.CompilerParams(
            collective_id=0, has_side_effects=True, vmem_limit_bytes=60 * 1024 * 1024
        ),
        cost_estimate=pl.CostEstimate(
            flops=16 * tile * D * 3 * HD, bytes_accessed=8 * tile * D, transcendentals=tile * tile
        ),
        name="recursion_sublayer",
    )(tile_depth, hidden_in, cotangent, w_qkv, w_out, gain[None, :])
    parts = [(i, slice(p * tile // 4, (p + 1) * tile // 4)) for i in (0, 1) for p in range(4)]
    parts += [(2, t) for t in range(3)] + [(3, slice(None))]
    anywhere = pl.BlockSpec(memory_space=pl.ANY)
    return pl.pallas_call(
        functools.partial(write_out, parts),
        out_shape=tuple(jax.ShapeDtypeStruct(r.shape, r.dtype) for r in results),
        in_specs=[anywhere] * 4,
        out_specs=(anywhere,) * 4,
        scratch_shapes=[pltpu.SemaphoreType.DMA((len(parts),))],
        name="write_outputs",
    )(*results)


def solution(mesh):
    in_specs = (
        P("dp", "context", None),
        P("dp", "context", None),
        P("dp", None),
        P(None, "dp", "context"),
        P("context", "dp"),
        P(),
    )
    out_specs = (
        P("dp", "context", None),
        P("dp", "context", None),
        P(None, "dp", "context"),
        P("context", "dp"),
    )
    return jax.shard_map(
        on_device, mesh=mesh, in_specs=in_specs, out_specs=out_specs, check_vma=False
    )
```

time: 408 us -> 109 us (0.27)
  waiting for transfers between devices: 294 us -> 0 us
  Pallas kernels: 0 us -> 108 us
  blocking collectives: 46 us -> 0 us
  other arithmetic: 22.5 us -> 0 us
  matrix products: 22.4 us -> 0 us
  between operations: 17.3 us -> 0.64 us
    reduce_scatter x2 -> x0, waiting for transfers between devices: 189 us -> none  [the longest x1 111 us: on_device(): lax.psum_scatter(total_qkv, 'dp', scatter_dimension=1, tiled=True)]
    pallas_call x0 -> x2, Pallas kernels: none -> 108 us  [the longest x1 66.7 us: on_device(): pl.pallas_call(functools.partial(kernel, dims, contexts, chunks, keys), o...]
    psum x6 -> x0, waiting for transfers between devices: 86.4 us -> none  [the longest x3 46.6 us: head_sum(): return lax.psum(terms.astype(jnp.bfloat16), 'context').astype(jnp.float32)]
    all_gather x1 -> x0, blocking collectives: 46 us -> none  [on_device(): lax.all_gather(w_out, 'dp', axis=1, tiled=True)]
    dot_general x24 -> x0, matrix products: 22.4 us -> none  [the longest x2 4.13 us: backward_level(): jnp.einsum('rd,trc->tdc', rows, dqkv, preferred_element_type=jnp.float32)]
    all_gather x1 -> x0, waiting for transfers between devices: 18.6 us -> none  [on_device(): lax.all_gather(w_qkv, 'dp', axis=1, tiled=True)]
    select_n x4 -> x0, other arithmetic: 8.61 us -> none  [from_root(): jnp.where(lax.axis_index(axis) == source, value, 0).astype(value.dtype)]
    reduce_sum x8 -> x0, other arithmetic: 7.28 us -> none  [the longest x2 3.33 us: forward_level(): inv = lax.rsqrt(jnp.mean(x32 * x32, -1, keepdims=True) + 1e-06)]
  transfers between devices with their start and end apart: 9 -> 0, of which waited for: 8 -> 0; matrix products, arithmetic and copies ran while one was open for 4% -> 0% of each run, Pallas kernels for 0% -> 0%
where the time goes in v1:
time: 109 us; the launch traced here: 108 us
  Pallas kernels  108 us (99%)
    pallas_call x1, Pallas kernels, on_device(): pl.pallas_call(functools.partial(kernel, dims, contexts, chunks, keys), o...  66.7 us
    pallas_call x1, Pallas kernels, on_device(): pl.pallas_call(functools.partial(write_out, parts), out_shape=tuple((jax....  40.9 us

profile of v1, /device:TPU:0, one launch (start us, length us, event | category | flops | bytes accessed | tf_op | source)
XLA Modules:
  0.0 108.3 jit_solution(11114572897925025961)
XLA Ops:
  0.6 66.7 %recursion_sublayer.1 = (bf16[1,128,2048]{2,1,0:T(8,128)(2,1)}, bf16[1,128,2048]{2,1,0:T(8,128)(2,1)}, f32[3,128,128]{2,1,0:T(8,128)}, f32[128,128]{1,0:T(8,128)}) custom-call(s32[1,2]{1,0:T(1,128)} %depth.1, bf16[1,128,2048]{2,1,0:T(8,128)(2,1)} %hid.1, bf16[1,128,2048]{2,1,0:T(8,128)(2,1)} %cot.1, bf16[3,128,128]{2,1,0:T(8,128)(2,1)} %wq.1, ...), custom_call_target="tpu_custom_call" | custom-call | flops 1610612736 | bytes 2097152 | tf_op jit(solution)/shard_map/recursion_sublayer/pallas_call | solution.py:427
  67.4 40.9 %write_outputs.1 = (bf16[1,128,2048]{2,1,0:T(8,128)(2,1)}, bf16[1,128,2048]{2,1,0:T(8,128)(2,1)}, f32[3,128,128]{2,1,0:T(8,128)}, f32[128,128]{1,0:T(8,128)}) custom-call(bf16[1,128,2048]{2,1,0:T(8,128)(2,1)} %get-tuple-element.8.refs_0_, bf16[1,128,2048]{2,1,0:T(8,128)(2,1)} %get-tuple-element.9.refs_1_, f32[3,128,128]{2,1,0:T(8,128)} %get-tuple-element.10.refs_2_, ...), custom_call_target="tpu_custom_call" | custom-call | tf_op jit(solution)/shard_map/write_outputs/pallas_call | solution.py:476

commit v2 on v1

--- a/solution.py
+++ b/solution.py
@@ -26,10 +26,8 @@
     Z, Y, X = dims
     first = (X, Y)
     second = (Y, X)
-    keys = []
-    for o in range(1, contexts):
-        keys += [("hid", o), ("cot", o)]
-        keys += [(name, o, j) for name in EXCHANGES for j in range(chunks)]
+    keys = [(name, o) for o in range(1, contexts) for name in ("hid", "cot")]
+    keys += [(n, o, j) for n in EXCHANGES for o in range(1, contexts) for j in range(chunks)]
     for h in range(2):
         keys += [("gz", h, oz) for oz in range(1, Z)]
         keys += [("g1", h, o1, oz) for o1 in range(1, first[h]) for oz in range(Z)]
@@ -39,6 +37,7 @@
             for o1 in range(first[h])
             for oz in range(Z)
         ]
+    for h in range(2):
         keys += [
             ("s1", h, o1, o2, oz)
             for o1 in range(1, second[h])
@@ -79,28 +78,36 @@
         place = list(me)
         for name, off in moves.items():
             axis = int(name[1])
-            place[axis] = lax.rem(me[axis] + off + dims[axis], dims[axis]) if off else me[axis]
+            if not (isinstance(off, int) and off == 0):
+                place[axis] = lax.rem(me[axis] + off + dims[axis], dims[axis])
         return (place[0] * Y + place[1]) * X + place[2]
 
     def at(axes):
         return spot(**{"a%d" % axis: off for axis, off in axes})
 
-    started = []
-
-    def copy(key, src, dst, peer):
-        number = keys[key]
+    def number_of(key):
+        low = 0 if (*key[:-1], 0) in keys else 1
+        return keys[(*key[:-1], low)] + (key[-1] - low)
+
+    def copy(number, src, dst, peer):
         return pltpu.make_async_remote_copy(
             src_ref=src, dst_ref=dst, send_sem=send_sem.at[number], recv_sem=recv_sem.at[number],
             device_id=peer, device_id_type=MESH,
         )
 
     def send(key, src, dst, peer):
-        c = copy(key, src, dst, peer)
-        c.start()
-        started.append(c)
+        copy(number_of(key), src, dst, peer).start()
+
+    def loop(low, high, body):
+        def step(i, carry):
+            body(i)
+            return carry
+
+        if high > low:
+            lax.fori_loop(low, high, step, 0)
 
     def arrive(key, dst):
-        copy(key, dst, dst, (dp, ctx)).wait_recv()
+        copy(number_of(key), dst, dst, (dp, ctx)).wait_recv()
 
     def ctx_peer(o):
         return (dp, lax.rem(ctx + o, contexts))
@@ -172,9 +179,13 @@
         slot = contexts - o - 1
         arrive(("hid", o), peer_h.at[slot])
         arrive(("cot", o), peer_g.at[slot])
-    cols = [pl.ds(j * width, width) for j in range(chunks)]
-    square = jnp.zeros((tile, 1), F32)
-    for c in cols:
+    no_rows = jnp.zeros((tile, 1), F32)
+
+    def col(j):
+        return pl.ds(pl.multiple_of(j * width, HD), width)
+
+    def take_live(j, square):
+        c = col(j)
         live_h = hid[0, :, c].astype(F32) * own2
         live_g = cot[0, :, c].astype(F32) * own2
         for s in range(contexts - 1):
@@ -184,18 +195,25 @@
         hL[:, c] = live_h.astype(BF)
         DY[0:tile, c] = live_g.astype(BF)
         DY[tile : 2 * tile, c] = (live_g * valid3).astype(BF)
-        square = square + jnp.sum(live_h * live_h, -1, keepdims=True)
+        return square + jnp.sum(live_h * live_h, -1, keepdims=True)
+
+    square = lax.fori_loop(0, chunks, take_live, no_rows)
     inv2 = lax.rsqrt(square * (1.0 / D) + 1e-06)
-    for c in cols:
+
+    @functools.partial(loop, 0, chunks)
+    def _(j):
+        c = col(j)
         R[0:tile, c] = (hL[:, c].astype(F32) * inv2 * gain[:, c]).astype(BF)
 
-    for oz in range(1, Z):
+    def from_z(oz):
         for h in range(2):
             arrive(("gz", h, oz), piece(h, [(0, -oz)]))
             spread_first(h, oz)
         for h in range(2):
             spread_second(h, oz, 0)
         pass_on(oz - 1)
+
+    loop(1, Z, from_z)
     pass_on(Z - 1)
 
     group = D // Z
@@ -203,7 +221,11 @@
     def group_of(oz):
         return pl.ds(pl.multiple_of(lax.rem(zz + oz + Z, Z) * group, group), group)
 
-    for oz in range(Z):
+    accA[...] = jnp.zeros_like(accA)
+    accB[...] = jnp.zeros_like(accB)
+
+    @functools.partial(loop, 0, Z)
+    def _(oz):
         for h in range(2):
             d1, d2 = order[h]
             for o1 in range(dims[d1]):
@@ -211,10 +233,8 @@
                     arrive(("g2", h, o2, o1, oz), piece(h, [(0, -oz), (d1, -o1), (d2, -o2)]))
         g = group_of(-oz)
         rows, grads = R[0:tile, g], DY[0:tile, g]
-        part_a = nn(rows, WA[g, :])
-        part_b = nn(jnp.concatenate([rows, grads], axis=0), WB[g, :])
-        accA[...] = part_a if oz == 0 else accA[...] + part_a
-        accB[...] = part_b if oz == 0 else accB[...] + part_b
+        accA[...] += nn(rows, WA[g, :])
+        accB[...] += nn(jnp.concatenate([rows, grads], axis=0), WB[g, :])
         WAT[:, g] = WA[g, :].T
         WBT[:, g] = WB[g, :].T
 
@@ -236,8 +256,10 @@
 
     def swap_out(name, term):
         e = EXCHANGES.index(name)
-        for j in range(chunks):
-            own_x[e, j] = term(cols[j]).astype(BF)
+
+        @functools.partial(loop, 0, chunks)
+        def _(j):
+            own_x[e, j] = term(col(j)).astype(BF)
             for o in range(1, contexts):
                 send((name, o, j), own_x.at[e, j], got_x.at[e, contexts - o - 1, j], ctx_peer(o))
 
@@ -263,17 +285,24 @@
     swap_out("mix2", lambda c: nn(keep2[5], WBT[HD : 2 * HD, c]))
     grad_out3 = accB[tile : 2 * tile, HD : 2 * HD]
     dattn3 = (grad_out3 * valid3).astype(BF)
-    square = jnp.zeros((tile, 1), F32)
-    qk3 = jnp.zeros((tile, 2 * HD), F32)
-    vo3 = jnp.zeros((2 * tile, 2 * HD), F32)
-    for j, c in enumerate(cols):
+
+    def take_mix2(j, carry):
+        square, qk, vo = carry
+        c = col(j)
         state = (hL[:, c].astype(F32) + swap_in("mix2", j)).astype(BF)
         h2[:, c] = state
         wide = state.astype(F32)
-        square = square + jnp.sum(wide * wide, -1, keepdims=True)
         gained = (wide * gain[:, c]).astype(BF)
-        qk3 = qk3 + nn(gained, WA[c, :])
-        vo3 = vo3 + nn(jnp.concatenate([gained, state], axis=0), WB[c, :])
+        return (
+            square + jnp.sum(wide * wide, -1, keepdims=True),
+            qk + nn(gained, WA[c, :]),
+            vo + nn(jnp.concatenate([gained, state], axis=0), WB[c, :]),
+        )
+
+    square, qk3, vo3 = lax.fori_loop(
+        0, chunks, take_mix2,
+        (no_rows, jnp.zeros((tile, 2 * HD), F32), jnp.zeros((2 * tile, 2 * HD), F32)),
+    )
     inv3 = lax.rsqrt(square * (1.0 / D) + 1e-06)
     state_out = vo3[tile : 2 * tile, HD : 2 * HD]
 
@@ -282,31 +311,37 @@
     dqk3, dv3 = backward(keep3, dattn3)
     swap_out("dn3", lambda c: nn(dqk3, WAT[:, c]) + nn(dv3, WBT[0:HD, c]))
     swap_out("mix3", lambda c: nn(keep3[5], WBT[HD : 2 * HD, c]))
-    for c in cols:
+
+    @functools.partial(loop, 0, chunks)
+    def _(j):
+        c = col(j)
         R[tile : 2 * tile, c] = (h2[:, c].astype(F32) * inv3 * gain[:, c] * valid3).astype(BF)
 
-    def norm_grad(name, state, inv, on, term):
-        dot = jnp.zeros((tile, 1), F32)
-        for j, c in enumerate(cols):
+    def norm_grad(name, state, inv, on, start, term):
+        def step(j, carry):
+            dot, back = carry
+            c = col(j)
             u = swap_in(name, j) * gain[:, c]
             scaled[:, c] = u
-            dot = dot + jnp.sum(u * state[:, c].astype(F32), -1, keepdims=True)
-            term(c, u)
-        return inv * on, inv * inv * inv * (dot * (1.0 / D)) * on
+            return dot + jnp.sum(u * state[:, c].astype(F32), -1, keepdims=True), term(c, u, back)
+
+        dot, back = lax.fori_loop(0, chunks, step, (no_rows, start))
+        return inv * on, inv * inv * inv * (dot * (1.0 / D)) * on, back
 
     def norm_apply(state, c, first, second):
         return scaled[:, c] * first - state[:, c].astype(F32) * second
 
-    back = [jnp.zeros((tile, HD), F32)]
-
-    def back_term(c, u):
-        back[0] = back[0] + nn(u.astype(BF), WB[c, HD : 2 * HD])
-
-    first, second = norm_grad("dn3", h2, inv3, valid3, back_term)
-    dattn2 = (grad_out3 + back[0] * first - state_out * second).astype(BF)
+    first3, second3, back = norm_grad(
+        "dn3", h2, inv3, valid3, jnp.zeros((tile, HD), F32),
+        lambda c, u, back: back + nn(u.astype(BF), WB[c, HD : 2 * HD]),
+    )
+    dattn2 = (grad_out3 + back * first3 - state_out * second3).astype(BF)
     dqk2, dv2 = backward(keep2, dattn2)
-    for c in cols:
-        DY[0:tile, c] = (DY[0:tile, c].astype(F32) + norm_apply(h2, c, first, second)).astype(BF)
+
+    @functools.partial(loop, 0, chunks)
+    def _(j):
+        c = col(j)
+        DY[0:tile, c] = (DY[0:tile, c].astype(F32) + norm_apply(h2, c, first3, second3)).astype(BF)
 
     left_a = jnp.concatenate([dqk2, dqk3], axis=0).T
     left_v = jnp.concatenate([dv2, dv3], axis=0).T
@@ -322,7 +357,9 @@
     def half_rows(h):
         return pl.ds(h * 2 * HD, 2 * HD)
 
-    for oz in (*range(1, Z), 0):
+    @functools.partial(loop, 0, Z)
+    def _(i):
+        oz = lax.rem(i + 1, Z)
         g = group_of(oz)
         z = lax.rem(zz + oz, Z)
         cut(pl.ds(0, 2 * HD), nn(left_a, R[:, g]), z)
@@ -341,7 +378,10 @@
     swap_out("dn2", lambda c: nn(dqk2, WAT[:, c]) + nn(dv2, WBT[0:HD, c]))
 
     not2 = 1.0 - own2
-    for j, c in enumerate(cols):
+
+    @functools.partial(loop, 0, chunks)
+    def _(j):
+        c = col(j)
         state = (h2[:, c].astype(F32) + swap_in("mix3", j)).astype(BF).astype(F32)
         hout[0, :, c] = (hid[0, :, c].astype(F32) * not2 + state * own2).astype(BF)
 
@@ -353,7 +393,9 @@
             total = total + got1[h][o1 - 1, o2, oz].astype(F32)
         return total
 
-    for oz in (*range(1, Z), 0):
+    @functools.partial(loop, 0, Z)
+    def _(i):
+        oz = lax.rem(i + 1, Z)
         for h in range(2):
             e2, e1 = order[h]
             for o2 in range(1, dims[e2]):
@@ -363,9 +405,12 @@
                     (at([(e2, o2)]), ctx),
                 )
 
-    first, second = norm_grad("dn2", hL, inv2, 1.0, lambda c, u: None)
-    for c in cols:
-        grad = DY[0:tile, c].astype(F32) + norm_apply(hL, c, first, second)
+    first2, second2, _ = norm_grad("dn2", hL, inv2, 1.0, 0, lambda c, u, back: back)
+
+    @functools.partial(loop, 0, chunks)
+    def _(j):
+        c = col(j)
+        grad = DY[0:tile, c].astype(F32) + norm_apply(hL, c, first2, second2)
         grad = grad.astype(BF).astype(F32)
         gout[0, :, c] = (cot[0, :, c].astype(F32) * not2 + grad * own2).astype(BF)
 
@@ -376,7 +421,8 @@
             total = total + got2[h][o2 - 1, oz].astype(F32)
         return total
 
-    for oz in range(1, Z):
+    @functools.partial(loop, 1, Z)
+    def _(oz):
         for h in range(2):
             T2[h, oz - 1] = second_total(h, oz).astype(BF)
             send(("s3", h, oz), T2.at[h, oz - 1], R3.at[h, oz - 1], (at([(0, oz)]), ctx))
@@ -390,18 +436,20 @@
     gqkv[2] = final[1][0:HD].T
     gwo[...] = final[1][HD : 2 * HD]
 
-    for c in started:
-        c.wait_send()
-
-
-def write_out(parts, *refs):
+    def sent(kinds, block):
+        numbers = [number for key, number in keys.items() if key[0] in kinds]
+        if numbers:
+            loop(min(numbers), max(numbers) + 1, lambda k: copy(k, block, block, (dp, ctx)).wait_send())
+
+    sent(("hid", "cot"), hid.at[0])
+    sent(EXCHANGES, own_x.at[0, 0])
+    sent(("gz", "g1", "g2"), piece(0, []))
+    sent(("s1", "s2", "s3"), T2.at[0, 0])
+
+
+def write_out(*refs):
     sources, targets, sems = refs[:4], refs[4:8], refs[8]
-    copies = []
-    for number, (i, part) in enumerate(parts):
-        index = (0, part) if i < 2 else part
-        copies.append(
-            pltpu.make_async_copy(sources[i].at[index], targets[i].at[index], sems.at[number])
-        )
+    copies = [pltpu.make_async_copy(sources[i], targets[i], sems.at[i]) for i in range(4)]
     for c in copies:
         c.start()
     for c in copies:
@@ -470,15 +518,12 @@
         ),
         name="recursion_sublayer",
     )(tile_depth, hidden_in, cotangent, w_qkv, w_out, gain[None, :])
-    parts = [(i, slice(p * tile // 4, (p + 1) * tile // 4)) for i in (0, 1) for p in range(4)]
-    parts += [(2, t) for t in range(3)] + [(3, slice(None))]
-    anywhere = pl.BlockSpec(memory_space=pl.ANY)
     return pl.pallas_call(
-        functools.partial(write_out, parts),
+        write_out,
         out_shape=tuple(jax.ShapeDtypeStruct(r.shape, r.dtype) for r in results),
-        in_specs=[anywhere] * 4,
-        out_specs=(anywhere,) * 4,
-        scratch_shapes=[pltpu.SemaphoreType.DMA((len(parts),))],
+        in_specs=[vmem] * 4,
+        out_specs=(pl.BlockSpec(memory_space=pl.ANY),) * 4,
+        scratch_shapes=[pltpu.SemaphoreType.DMA((4,))],
         name="write_outputs",
     )(*results)
 

time: 109 us -> 71.4 us (0.66)
  Pallas kernels: 108 us -> 70.1 us
    pallas_call x1, Pallas kernels: 40.9 us -> 2.32 us  [on_device(): pl.pallas_call(write_out, out_shape=tuple((jax.ShapeDtypeStruct(r.shape,...]
    pallas_call x1, Pallas kernels: 66.7 us -> 67.8 us  [on_device(): pl.pallas_call(functools.partial(kernel, dims, contexts, chunks, keys), o...]
where the time goes in v2:
time: 71.4 us; the launch traced here: 70.8 us
  Pallas kernels  70.1 us (98%)
    pallas_call x1, Pallas kernels, on_device(): pl.pallas_call(functools.partial(kernel, dims, contexts, chunks, keys), o...  67.8 us
    pallas_call x1, Pallas kernels, on_device(): pl.pallas_call(write_out, out_shape=tuple((jax.ShapeDtypeStruct(r.shape,...  2.32 us

profile of v2, /device:TPU:0, one launch (start us, length us, event | category | flops | bytes accessed | tf_op | source)
XLA Modules:
  0.0 70.8 jit_solution(1652950459830420142)
XLA Ops:
  0.6 67.8 %recursion_sublayer.1 = (bf16[1,128,2048]{2,1,0:T(8,128)(2,1)}, bf16[1,128,2048]{2,1,0:T(8,128)(2,1)}, f32[3,128,128]{2,1,0:T(8,128)}, f32[128,128]{1,0:T(8,128)}) custom-call(s32[1,2]{1,0:T(1,128)} %depth.1, bf16[1,128,2048]{2,1,0:T(8,128)(2,1)} %hid.1, bf16[1,128,2048]{2,1,0:T(8,128)(2,1)} %cot.1, bf16[3,128,128]{2,1,0:T(8,128)(2,1)} %wq.1, ...), custom_call_target="tpu_custom_call" | custom-call | flops 1610612736 | bytes 2097152 | tf_op jit(solution)/shard_map/recursion_sublayer/pallas_call | solution.py:475
  68.4 2.3 %write_outputs.1 = (bf16[1,128,2048]{2,1,0:T(8,128)(2,1)}, bf16[1,128,2048]{2,1,0:T(8,128)(2,1)}, f32[3,128,128]{2,1,0:T(8,128)}, f32[128,128]{1,0:T(8,128)}) custom-call(bf16[1,128,2048]{2,1,0:T(8,128)(2,1)} %get-tuple-element.8.refs_0_, bf16[1,128,2048]{2,1,0:T(8,128)(2,1)} %get-tuple-element.9.refs_1_, f32[3,128,128]{2,1,0:T(8,128)} %get-tuple-element.10.refs_2_, ...), custom_call_target="tpu_custom_call" | custom-call | tf_op jit(solution)/shard_map/write_outputs/pallas_call | solution.py:521

commit v3 on v2

--- a/solution.py
+++ b/solution.py
@@ -30,6 +30,7 @@
     keys += [(n, o, j) for n in EXCHANGES for o in range(1, contexts) for j in range(chunks)]
     for h in range(2):
         keys += [("gz", h, oz) for oz in range(1, Z)]
+        keys += [(way, h, step) for way in ("up", "down") for step in range(Z - 1)]
         keys += [("g1", h, o1, oz) for o1 in range(1, first[h]) for oz in range(Z)]
         keys += [
             ("g2", h, o2, o1, oz)
@@ -89,14 +90,16 @@
         low = 0 if (*key[:-1], 0) in keys else 1
         return keys[(*key[:-1], low)] + (key[-1] - low)
 
-    def copy(number, src, dst, peer):
+    def copy(number, src, dst, peer, leaving=None):
+        leaving = number if leaving is None else leaving
         return pltpu.make_async_remote_copy(
-            src_ref=src, dst_ref=dst, send_sem=send_sem.at[number], recv_sem=recv_sem.at[number],
+            src_ref=src, dst_ref=dst, send_sem=send_sem.at[leaving], recv_sem=recv_sem.at[number],
             device_id=peer, device_id_type=MESH,
         )
 
-    def send(key, src, dst, peer):
-        copy(number_of(key), src, dst, peer).start()
+    def send(key, src, dst, peer, leaving=None):
+        leaving = None if leaving is None else number_of(leaving)
+        copy(number_of(key), src, dst, peer, leaving).start()
 
     def loop(low, high, body):
         def step(i, carry):
@@ -131,14 +134,17 @@
         p = at(axes)
         return halves[h].at[pl.ds(pl.multiple_of(p * dloc, dloc), dloc), :]
 
-    for h in range(2):
-        for oz in range(1, Z):
-            block = piece(h, [])
-            send(("gz", h, oz), block, block, (at([(0, oz)]), ctx))
-    for o in range(1, contexts):
-        slot = contexts - o - 1
-        send(("hid", o), hid.at[0], peer_h.at[slot], ctx_peer(o))
-        send(("cot", o), cot.at[0], peer_g.at[slot], ctx_peer(o))
+    def line_up(h, step):
+        @pl.when((zz >= step) & (zz < Z - 1))
+        def _():
+            block = piece(h, [(0, -step)])
+            send(("gz", h, step + 1), block, block, (at([(0, 1)]), ctx), ("up", h, step))
+
+    def line_down(h, step):
+        @pl.when((zz + step <= Z - 1) & (zz > 0))
+        def _():
+            block = piece(h, [(0, step)])
+            send(("gz", h, Z - 1 - step), block, block, (at([(0, -1)]), ctx), ("down", h, step))
 
     def spread_first(h, oz):
         d1 = order[h][0]
@@ -161,8 +167,15 @@
 
     for h in range(2):
         spread_first(h, 0)
+        if Z > 1:
+            line_up(h, 0)
+            line_down(h, 0)
     for h in range(2):
         spread_second(h, 0, 0)
+    for o in range(1, contexts):
+        slot = contexts - o - 1
+        send(("hid", o), hid.at[0], peer_h.at[slot], ctx_peer(o))
+        send(("cot", o), cot.at[0], peer_g.at[slot], ctx_peer(o))
 
     tiles = depth.shape[1]
 
@@ -205,16 +218,33 @@
         c = col(j)
         R[0:tile, c] = (hL[:, c].astype(F32) * inv2 * gain[:, c]).astype(BF)
 
-    def from_z(oz):
+    def from_z(oz, step, line):
         for h in range(2):
             arrive(("gz", h, oz), piece(h, [(0, -oz)]))
             spread_first(h, oz)
+
+            @pl.when(step < Z - 1)
+            def _(h=h):
+                line(h, step)
+
         for h in range(2):
             spread_second(h, oz, 0)
-        pass_on(oz - 1)
-
-    loop(1, Z, from_z)
-    pass_on(Z - 1)
+
+    def both_ways(step, act):
+        @pl.when(zz >= step)
+        def _():
+            act(step, line_up)
+
+        @pl.when(zz + step <= Z - 1)
+        def _():
+            act(Z - step, line_down)
+
+    pass_on(0)
+
+    @functools.partial(loop, 1, Z)
+    def _(step):
+        both_ways(step, lambda oz, line: from_z(oz, step, line))
+        both_ways(step, lambda oz, line: pass_on(oz))
 
     group = D // Z
 
@@ -224,8 +254,7 @@
     accA[...] = jnp.zeros_like(accA)
     accB[...] = jnp.zeros_like(accB)
 
-    @functools.partial(loop, 0, Z)
-    def _(oz):
+    def project(oz):
         for h in range(2):
             d1, d2 = order[h]
             for o1 in range(dims[d1]):
@@ -237,6 +266,12 @@
         accB[...] += nn(jnp.concatenate([rows, grads], axis=0), WB[g, :])
         WAT[:, g] = WA[g, :].T
         WBT[:, g] = WB[g, :].T
+
+    project(0)
+
+    @functools.partial(loop, 1, Z)
+    def _(step):
+        both_ways(step, lambda oz, line: project(oz))
 
     causal = lax.broadcasted_iota(jnp.int32, (tile, tile), 1) <= lax.broadcasted_iota(
         jnp.int32, (tile, tile), 0
@@ -357,9 +392,12 @@
     def half_rows(h):
         return pl.ds(h * 2 * HD, 2 * HD)
 
+    def nth(i):
+        return jnp.where(2 * zz < Z, Z - 1 - i, lax.rem(i + 1, Z))
+
     @functools.partial(loop, 0, Z)
     def _(i):
-        oz = lax.rem(i + 1, Z)
+        oz = nth(i)
         g = group_of(oz)
         z = lax.rem(zz + oz, Z)
         cut(pl.ds(0, 2 * HD), nn(left_a, R[:, g]), z)
@@ -377,14 +415,6 @@
                     )
     swap_out("dn2", lambda c: nn(dqk2, WAT[:, c]) + nn(dv2, WBT[0:HD, c]))
 
-    not2 = 1.0 - own2
-
-    @functools.partial(loop, 0, chunks)
-    def _(j):
-        c = col(j)
-        state = (h2[:, c].astype(F32) + swap_in("mix3", j)).astype(BF).astype(F32)
-        hout[0, :, c] = (hid[0, :, c].astype(F32) * not2 + state * own2).astype(BF)
-
     def first_total(h, o2, oz):
         e2, e1 = order[h]
         total = G[at([(0, oz), (e2, o2)]), half_rows(h), :].astype(F32)
@@ -393,9 +423,7 @@
             total = total + got1[h][o1 - 1, o2, oz].astype(F32)
         return total
 
-    @functools.partial(loop, 0, Z)
-    def _(i):
-        oz = lax.rem(i + 1, Z)
+    def second_phase(oz):
         for h in range(2):
             e2, e1 = order[h]
             for o2 in range(1, dims[e2]):
@@ -405,6 +433,33 @@
                     (at([(e2, o2)]), ctx),
                 )
 
+    def second_total(h, oz):
+        total = first_total(h, 0, oz)
+        for o2 in range(1, dims[order[h][0]]):
+            arrive(("s2", h, o2, oz), got2[h].at[o2 - 1, oz])
+            total = total + got2[h][o2 - 1, oz].astype(F32)
+        return total
+
+    def third_phase(oz):
+        for h in range(2):
+            T2[h, oz - 1] = second_total(h, oz).astype(BF)
+            send(("s3", h, oz), T2.at[h, oz - 1], R3.at[h, oz - 1], (at([(0, oz)]), ctx))
+
+    second_phase(nth(0))
+
+    @functools.partial(loop, 1, Z)
+    def _(i):
+        second_phase(nth(i))
+        third_phase(nth(i - 1))
+
+    not2 = 1.0 - own2
+
+    @functools.partial(loop, 0, chunks)
+    def _(j):
+        c = col(j)
+        state = (h2[:, c].astype(F32) + swap_in("mix3", j)).astype(BF).astype(F32)
+        hout[0, :, c] = (hid[0, :, c].astype(F32) * not2 + state * own2).astype(BF)
+
     first2, second2, _ = norm_grad("dn2", hL, inv2, 1.0, 0, lambda c, u, back: back)
 
     @functools.partial(loop, 0, chunks)
@@ -414,18 +469,6 @@
         grad = grad.astype(BF).astype(F32)
         gout[0, :, c] = (cot[0, :, c].astype(F32) * not2 + grad * own2).astype(BF)
 
-    def second_total(h, oz):
-        total = first_total(h, 0, oz)
-        for o2 in range(1, dims[order[h][0]]):
-            arrive(("s2", h, o2, oz), got2[h].at[o2 - 1, oz])
-            total = total + got2[h][o2 - 1, oz].astype(F32)
-        return total
-
-    @functools.partial(loop, 1, Z)
-    def _(oz):
-        for h in range(2):
-            T2[h, oz - 1] = second_total(h, oz).astype(BF)
-            send(("s3", h, oz), T2.at[h, oz - 1], R3.at[h, oz - 1], (at([(0, oz)]), ctx))
     final = [second_total(h, 0) for h in range(2)]
     for h in range(2):
         for oz in range(1, Z):
@@ -436,14 +479,29 @@
     gqkv[2] = final[1][0:HD].T
     gwo[...] = final[1][HD : 2 * HD]
 
-    def sent(kinds, block):
-        numbers = [number for key, number in keys.items() if key[0] in kinds]
+    def sent(kinds, block, half=None):
+        numbers = [
+            number for key, number in keys.items() if key[0] in kinds and half in (None, key[1])
+        ]
         if numbers:
             loop(min(numbers), max(numbers) + 1, lambda k: copy(k, block, block, (dp, ctx)).wait_send())
 
     sent(("hid", "cot"), hid.at[0])
     sent(EXCHANGES, own_x.at[0, 0])
-    sent(("gz", "g1", "g2"), piece(0, []))
+    for h in range(2):
+        sent(("g1", "g2"), piece(0, []), h)
+
+    def line_sent(way, step, on):
+        @pl.when(on)
+        def _():
+            for h in range(2):
+                copy(number_of((way, h, step)), piece(h, []), piece(h, []), (dp, ctx)).wait_send()
+
+    @functools.partial(loop, 0, Z - 1)
+    def _(step):
+        line_sent("up", step, (zz >= step) & (zz < Z - 1))
+        line_sent("down", step, (zz + step <= Z - 1) & (zz > 0))
+
     sent(("s1", "s2", "s3"), T2.at[0, 0])
 
 

time: 71.4 us -> 68.2 us (0.955)
  Pallas kernels: 70.1 us -> 67.4 us
    pallas_call x1, Pallas kernels: 67.8 us -> 65.1 us  [on_device(): pl.pallas_call(functools.partial(kernel, dims, contexts, chunks, keys), o...]
where the time goes in v3:
time: 68.2 us; the launch traced here: 68 us
  Pallas kernels  67.4 us (99%)
    pallas_call x1, Pallas kernels, on_device(): pl.pallas_call(functools.partial(kernel, dims, contexts, chunks, keys), o...  65.1 us
    pallas_call x1, Pallas kernels, on_device(): pl.pallas_call(write_out, out_shape=tuple((jax.ShapeDtypeStruct(r.shape,...  2.32 us

profile of v3, /device:TPU:0, one launch (start us, length us, event | category | flops | bytes accessed | tf_op | source)
XLA Modules:
  0.0 68.0 jit_solution(2557938247228471643)
XLA Ops:
  0.6 65.1 %recursion_sublayer.1 = (bf16[1,128,2048]{2,1,0:T(8,128)(2,1)}, bf16[1,128,2048]{2,1,0:T(8,128)(2,1)}, f32[3,128,128]{2,1,0:T(8,128)}, f32[128,128]{1,0:T(8,128)}) custom-call(s32[1,2]{1,0:T(1,128)} %depth.1, bf16[1,128,2048]{2,1,0:T(8,128)(2,1)} %hid.1, bf16[1,128,2048]{2,1,0:T(8,128)(2,1)} %cot.1, bf16[3,128,128]{2,1,0:T(8,128)(2,1)} %wq.1, ...), custom_call_target="tpu_custom_call" | custom-call | flops 1610612736 | bytes 2097152 | tf_op jit(solution)/shard_map/recursion_sublayer/pallas_call | solution.py:533
  65.7 2.3 %write_outputs.1 = (bf16[1,128,2048]{2,1,0:T(8,128)(2,1)}, bf16[1,128,2048]{2,1,0:T(8,128)(2,1)}, f32[3,128,128]{2,1,0:T(8,128)}, f32[128,128]{1,0:T(8,128)}) custom-call(bf16[1,128,2048]{2,1,0:T(8,128)(2,1)} %get-tuple-element.8.refs_0_, bf16[1,128,2048]{2,1,0:T(8,128)(2,1)} %get-tuple-element.9.refs_1_, f32[3,128,128]{2,1,0:T(8,128)} %get-tuple-element.10.refs_2_, ...), custom_call_target="tpu_custom_call" | custom-call | tf_op jit(solution)/shard_map/write_outputs/pallas_call | solution.py:579

commit v4 on v3

--- a/solution.py
+++ b/solution.py
@@ -60,11 +60,19 @@
 
 def kernel(
     dims, contexts, chunks, keys,
-    depth, hid, cot, wq, wo, gain,
+    depth_in, hid_in, cot_in, wq_in, wo_in, gain_in,
     hout, gout, gqkv, gwo,
     WA, WB, WAT, WBT, accA, accB, peer_h, peer_g, hL, h2, R, DY, scaled, own_x, got_x,
-    G, R1a, R1b, R2a, R2b, R3, T1a, T1b, T2, send_sem, recv_sem,
+    G, R1a, R1b, R2a, R2b, R3, T1a, T1b, T2, depth, hid, cot, wq, wo, gain, load_sem, send_sem, recv_sem,
 ):
+    loads = [
+        pltpu.make_async_copy(source, target, load_sem.at[i])
+        for i, (source, target) in enumerate((
+            (wq_in, wq), (wo_in, wo), (hid_in, hid), (cot_in, cot), (gain_in, gain), (depth_in, depth),
+        ))
+    ]
+    for load in loads:
+        load.start()
     Z, Y, X = dims
     dp = lax.axis_index("dp")
     ctx = lax.axis_index("context")
@@ -121,6 +129,8 @@
     for peer in peers:
         pl.semaphore_signal(barrier, inc=1, device_id=peer, device_id_type=MESH)
 
+    loads[0].wait()
+    loads[1].wait()
     mine = pl.ds(pl.multiple_of(dp * dloc, dloc), dloc)
     WA[mine, 0:HD] = wq[0]
     WA[mine, HD : 2 * HD] = wq[1]
@@ -172,10 +182,41 @@
             line_down(h, 0)
     for h in range(2):
         spread_second(h, 0, 0)
+    for load in loads[2:]:
+        load.wait()
     for o in range(1, contexts):
         slot = contexts - o - 1
         send(("hid", o), hid.at[0], peer_h.at[slot], ctx_peer(o))
         send(("cot", o), cot.at[0], peer_g.at[slot], ctx_peer(o))
+
+    def from_z(oz, step, line):
+        for h in range(2):
+            arrive(("gz", h, oz), piece(h, [(0, -oz)]))
+            spread_first(h, oz)
+
+            @pl.when(step < Z - 1)
+            def _(h=h):
+                line(h, step)
+
+        for h in range(2):
+            spread_second(h, oz, 0)
+
+    def both_ways(step, act):
+        @pl.when(zz >= step)
+        def _():
+            act(step, line_up)
+
+        @pl.when(zz + step <= Z - 1)
+        def _():
+            act(Z - step, line_down)
+
+    pass_on(0)
+
+    def z_step(step):
+        both_ways(step, lambda oz, line: from_z(oz, step, line))
+        both_ways(step, lambda oz, line: pass_on(oz))
+
+    loop(1, min(2, Z), z_step)
 
     tiles = depth.shape[1]
 
@@ -218,33 +259,7 @@
         c = col(j)
         R[0:tile, c] = (hL[:, c].astype(F32) * inv2 * gain[:, c]).astype(BF)
 
-    def from_z(oz, step, line):
-        for h in range(2):
-            arrive(("gz", h, oz), piece(h, [(0, -oz)]))
-            spread_first(h, oz)
-
-            @pl.when(step < Z - 1)
-            def _(h=h):
-                line(h, step)
-
-        for h in range(2):
-            spread_second(h, oz, 0)
-
-    def both_ways(step, act):
-        @pl.when(zz >= step)
-        def _():
-            act(step, line_up)
-
-        @pl.when(zz + step <= Z - 1)
-        def _():
-            act(Z - step, line_down)
-
-    pass_on(0)
-
-    @functools.partial(loop, 1, Z)
-    def _(step):
-        both_ways(step, lambda oz, line: from_z(oz, step, line))
-        both_ways(step, lambda oz, line: pass_on(oz))
+    loop(2, Z, z_step)
 
     group = D // Z
 
@@ -345,7 +360,6 @@
     keep3 = attend(qk3 * factor3, vo3[0:tile, 0:HD] * factor3, valid3)
     dqk3, dv3 = backward(keep3, dattn3)
     swap_out("dn3", lambda c: nn(dqk3, WAT[:, c]) + nn(dv3, WBT[0:HD, c]))
-    swap_out("mix3", lambda c: nn(keep3[5], WBT[HD : 2 * HD, c]))
 
     @functools.partial(loop, 0, chunks)
     def _(j):
@@ -413,6 +427,7 @@
                         got1[h].at[o1 - 1, o2, oz],
                         (at([(e1, o1)]), ctx),
                     )
+    swap_out("mix3", lambda c: nn(keep3[5], WBT[HD : 2 * HD, c]))
     swap_out("dn2", lambda c: nn(dqk2, WAT[:, c]) + nn(dv2, WBT[0:HD, c]))
 
     def first_total(h, o2, oz):
@@ -533,12 +548,12 @@
     results = pl.pallas_call(
         functools.partial(kernel, dims, contexts, chunks, keys),
         out_shape=(
-            jax.ShapeDtypeStruct(hidden_in.shape, BF),
-            jax.ShapeDtypeStruct(cotangent.shape, BF),
-            jax.ShapeDtypeStruct(w_qkv.shape, F32),
-            jax.ShapeDtypeStruct(w_out.shape, F32),
+            pltpu.VMEM(hidden_in.shape, BF),
+            pltpu.VMEM(cotangent.shape, BF),
+            pltpu.VMEM(w_qkv.shape, F32),
+            pltpu.VMEM(w_out.shape, F32),
         ),
-        in_specs=[pl.BlockSpec(memory_space=pltpu.SMEM)] + [vmem] * 5,
+        in_specs=[pl.BlockSpec(memory_space=pltpu.HBM)] * 6,
         out_specs=(vmem,) * 4,
         scratch_shapes=[
             pltpu.VMEM((D, 2 * HD), BF),
@@ -565,11 +580,18 @@
             block(X - 1, Z),
             block(Y - 1, Z),
             block(2, Z - 1),
+            pltpu.SMEM(tile_depth.shape, jnp.int32),
+            pltpu.VMEM(hidden_in.shape, BF),
+            pltpu.VMEM(cotangent.shape, BF),
+            pltpu.VMEM(w_qkv.shape, BF),
+            pltpu.VMEM(w_out.shape, BF),
+            pltpu.VMEM((1, D), F32),
+            pltpu.SemaphoreType.DMA((6,)),
             pltpu.SemaphoreType.DMA((len(keys),)),
             pltpu.SemaphoreType.DMA((len(keys),)),
         ],
         compiler_params=pltpu.CompilerParams(
-            collective_id=0, has_side_effects=True, vmem_limit_bytes=60 * 1024 * 1024
+            collective_id=0, has_side_effects=True, vmem_limit_bytes=56 * 1024 * 1024
         ),
         cost_estimate=pl.CostEstimate(
             flops=16 * tile * D * 3 * HD, bytes_accessed=8 * tile * D, transcendentals=tile * tile

time: 68.2 us -> 67.7 us (level)
  Pallas kernels: 67.4 us -> 64 us
  local copies, waits for them, and re-layouts: 0 us -> 2.88 us
    pallas_call x1, Pallas kernels: 65.1 us -> 61.7 us  [on_device(): pl.pallas_call(functools.partial(kernel, dims, contexts, chunks, keys), o...]
    unnamed x0 -> x8, local copies, waits for them, and re-layouts: none -> 2.88 us
where the time goes in v4:
time: 67.7 us; the launch traced here: 67.5 us
  Pallas kernels  64 us (95%)
  local copies, waits for them, and re-layouts  2.88 us (4%)
    pallas_call x1, Pallas kernels, on_device(): pl.pallas_call(functools.partial(kernel, dims, contexts, chunks, keys), o...  61.7 us
    unnamed x8, local copies, waits for them, and re-layouts  2.88 us
    pallas_call x1, Pallas kernels, on_device(): pl.pallas_call(write_out, out_shape=tuple((jax.ShapeDtypeStruct(r.shape,...  2.32 us

profile of v4, /device:TPU:0, one launch (start us, length us, event | category | flops | bytes accessed | tf_op | source)
XLA Modules:
  0.0 67.5 jit_solution(7553750081703482668)
XLA Ops:
  0.6 61.7 %recursion_sublayer.1 = (bf16[1,128,2048]{2,1,0:T(8,128)(2,1)S(1)}, bf16[1,128,2048]{2,1,0:T(8,128)(2,1)S(1)}, f32[3,128,128]{2,1,0:T(8,128)S(1)}, f32[128,128]{1,0:T(8,128)S(1)}) custom-call(s32[1,2]{1,0:T(1,128)} %depth_in.1, bf16[1,128,2048]{2,1,0:T(8,128)(2,1)} %hid_in.1, bf16[1,128,2048]{2,1,0:T(8,128)(2,1)} %cot_in.1, bf16[3,128,128]{2,1,0:T(8,128)(2,1)} %wq_in.1, ...), custom_call_target="tpu_custom_call" | custom-call | flops 1610612736 | bytes 2097152 | tf_op jit(solution)/shard_map/recursion_sublayer/pallas_call | solution.py:548
  62.3 0.0 copy-start
  62.3 0.8 %copy-done = bf16[1,128,2048]{2,1,0:T(8,128)(2,1)} copy-done((bf16[1,128,2048]{2,1,0:T(8,128)(2,1)}, bf16[1,128,2048]{2,1,0:T(8,128)(2,1)S(1)}, u32[]{:S(2)}) %copy-start) | copy-done | bytes 524312
  63.1 0.0 copy-start.1
  63.1 0.8 %copy-done.1 = bf16[1,128,2048]{2,1,0:T(8,128)(2,1)} copy-done((bf16[1,128,2048]{2,1,0:T(8,128)(2,1)}, bf16[1,128,2048]{2,1,0:T(8,128)(2,1)S(1)}, u32[]{:S(2)}) %copy-start.1) | copy-done | bytes 524312
  63.9 0.0 copy-start.2
  63.9 0.7 %copy-done.2 = f32[3,128,128]{2,1,0:T(8,128)} copy-done((f32[3,128,128]{2,1,0:T(8,128)}, f32[3,128,128]{2,1,0:T(8,128)S(1)}, u32[]{:S(2)}) %copy-start.2) | copy-done | bytes 196632
  64.6 0.0 copy-start.3
  64.6 0.6 copy-done.3
  65.2 2.3 %write_outputs.1 = (bf16[1,128,2048]{2,1,0:T(8,128)(2,1)}, bf16[1,128,2048]{2,1,0:T(8,128)(2,1)}, f32[3,128,128]{2,1,0:T(8,128)}, f32[128,128]{1,0:T(8,128)}) custom-call(bf16[1,128,2048]{2,1,0:T(8,128)(2,1)} %copy-done, bf16[1,128,2048]{2,1,0:T(8,128)(2,1)} %copy-done.1, f32[3,128,128]{2,1,0:T(8,128)} %copy-done.2, f32[128,128]{1,0:T(8,128)} %copy-done.3), custom_call_target="tpu_custom_call" | custom-call | tf_op jit(solution)/shard_map/write_outputs/pallas_call | solution.py:601
Async XLA Ops:
  62.3 0.8 %copy-start = (bf16[1,128,2048]{2,1,0:T(8,128)(2,1)}, bf16[1,128,2048]{2,1,0:T(8,128)(2,1)S(1)}, u32[]{:S(2)}) copy-start(bf16[1,128,2048]{2,1,0:T(8,128)(2,1)S(1)} %get-tuple-element.8.refs_0_) | copy-start | bytes 1572868
  63.1 0.8 %copy-start.1 = (bf16[1,128,2048]{2,1,0:T(8,128)(2,1)}, bf16[1,128,2048]{2,1,0:T(8,128)(2,1)S(1)}, u32[]{:S(2)}) copy-start(bf16[1,128,2048]{2,1,0:T(8,128)(2,1)S(1)} %get-tuple-element.9.refs_1_) | copy-start | bytes 1572868
  63.9 0.7 %copy-start.2 = (f32[3,128,128]{2,1,0:T(8,128)}, f32[3,128,128]{2,1,0:T(8,128)S(1)}, u32[]{:S(2)}) copy-start(f32[3,128,128]{2,1,0:T(8,128)S(1)} %get-tuple-element.10.refs_2_) | copy-start | bytes 589828
  64.6 0.6 copy-start.3

commit v5 on v4

--- a/solution.py
+++ b/solution.py
@@ -604,6 +604,7 @@
         in_specs=[vmem] * 4,
         out_specs=(pl.BlockSpec(memory_space=pl.ANY),) * 4,
         scratch_shapes=[pltpu.SemaphoreType.DMA((4,))],
+        compiler_params=pltpu.CompilerParams(vmem_limit_bytes=4 * 1024 * 1024),
         name="write_outputs",
     )(*results)
 

time: 67.7 us -> 63.5 us (0.938)
  local copies, waits for them, and re-layouts: 2.88 us -> 0 us
  Pallas kernels: 64 us -> 62.7 us
    unnamed x8 -> x0, local copies, waits for them, and re-layouts: 2.88 us -> none
    pallas_call x1, Pallas kernels: 2.32 us -> 1.08 us  [on_device(): pl.pallas_call(write_out, out_shape=tuple((jax.ShapeDtypeStruct(r.shape,...]
where the time goes in v5:
time: 63.5 us; the launch traced here: 63.4 us
  Pallas kernels  62.7 us (99%)
  between operations  0.64 us (1%)
    pallas_call x1, Pallas kernels, on_device(): pl.pallas_call(functools.partial(kernel, dims, contexts, chunks, keys), o...  61.7 us

profile of v5, /device:TPU:0, one launch (start us, length us, event | category | flops | bytes accessed | tf_op | source)
XLA Modules:
  0.0 63.4 jit_solution(829515278829137768)
XLA Ops:
  0.6 61.7 %recursion_sublayer.1 = (bf16[1,128,2048]{2,1,0:T(8,128)(2,1)S(1)}, bf16[1,128,2048]{2,1,0:T(8,128)(2,1)S(1)}, f32[3,128,128]{2,1,0:T(8,128)S(1)}, f32[128,128]{1,0:T(8,128)S(1)}) custom-call(s32[1,2]{1,0:T(1,128)} %depth_in.1, bf16[1,128,2048]{2,1,0:T(8,128)(2,1)} %hid_in.1, bf16[1,128,2048]{2,1,0:T(8,128)(2,1)} %cot_in.1, bf16[3,128,128]{2,1,0:T(8,128)(2,1)} %wq_in.1, ...), custom_call_target="tpu_custom_call" | custom-call | flops 1610612736 | bytes 2097152 | tf_op jit(solution)/shard_map/recursion_sublayer/pallas_call | solution.py:548
  62.3 1.1 %write_outputs.1 = (bf16[1,128,2048]{2,1,0:T(8,128)(2,1)}, bf16[1,128,2048]{2,1,0:T(8,128)(2,1)}, f32[3,128,128]{2,1,0:T(8,128)}, f32[128,128]{1,0:T(8,128)}) custom-call(bf16[1,128,2048]{2,1,0:T(8,128)(2,1)S(1)} %get-tuple-element.8.refs_0_, bf16[1,128,2048]{2,1,0:T(8,128)(2,1)S(1)} %get-tuple-element.9.refs_1_, ...), custom_call_target="tpu_custom_call" | custom-call | tf_op jit(solution)/shard_map/write_outputs/pallas_call | solution.py:601
